TPU v7x, 32 devices: a whole 2x2x4 slice. The times are simulated.
32 devices in a mesh: clip: 16 (over z, y, core), seq: 2 (over x).
Axes of the slice: x: 2, y: 2, z: 4, core: 2. Of those that a mesh axis runs over, the one named last changes fastest.
Arguments:
- query_rows: bfloat16 [16, 384, 5120], P('clip', 'seq'), may hold values from -32 to 32
- key_rows: bfloat16 [16, 384, 5120], P('clip', 'seq'), may hold values from -32 to 32
- value_rows: bfloat16 [16, 384, 5120], P('clip', 'seq'), may hold values from -6 to 6
- query_gain: float32 [5120], replicated, may hold values from 0.1 to 1.9
- key_gain: float32 [5120], replicated, may hold values from 0.1 to 1.9
- tile_lists: int32 [16, 40, 3, 3], P(None, 'seq'), may hold values from 0 to 2, as said below
- tile_counts: int32 [16, 40, 3], P(None, 'seq'), may hold values from 1 to 3, as said below
Outputs:
- attended: bfloat16 [16, 384, 5120], P('clip', 'seq')
Inputs may be any that keep to these rules, and one draw needn't show every extreme that they name: Each row tile_lists[c, h, b] is a permutation of 0 to 2 whose first entry is b; only its first tile_counts[c, h, b] entries are used. `tile_counts`: some entry equals 3 in every draw.
All inputs are finite; a program needn't handle non-finite values.
Results may differ from a plain program's by a relative error of at most 0.012.
The roundings to bfloat16 on the way count: a program that leaves them out, or rounds other values in their place, can miss the bound.
Values may be sent and summed in bfloat16 or wider, within the bound.
A program may use at most 128 MiB of HBM per device.

v0:
```python
import functools
import math

import jax
import jax.numpy as jnp
from jax import lax
from jax.experimental import pallas as pl
from jax.experimental.pallas import tpu as pltpu
from jax.sharding import PartitionSpec as P

HD = 128
BLK = 128
PAIR = 2
AHEAD = 3
NORM_ROWS = 16
MASKED = -1e30
EPSILON = 1e-06

MESH = pl.DeviceIdType.MESH


def kernel(
    n,
    query_hbm,
    key_hbm,
    value_hbm,
    query_gain,
    key_gain,
    lists,
    counts,
    out_hbm,
    query_buf,
    key_buf,
    value_buf,
    out_buf,
    codes,
    codes_smem,
    load_sem,
    send_sem,
    recv_sem,
    code_send_sem,
    code_recv_sem,
    code_load_sem,
    out_sem,
):
    tokens, width = query_buf.shape
    head_count = width // HD
    own_heads = lists.shape[3]
    block_count = lists.shape[0]
    groups = head_count // PAIR
    group_width = PAIR * HD
    row_group = math.gcd(tokens, BLK)
    me = lax.axis_index("seq")
    clip = lax.axis_index("clip")

    def rows_of(device):
        return pl.ds(pl.multiple_of(device * tokens, row_group), tokens)

    def columns_of(group):
        return pl.ds(pl.multiple_of(group * group_width, group_width), group_width)

    key_load = pltpu.make_async_copy(key_hbm.at[0], key_buf.at[rows_of(me)], load_sem.at[0])
    query_load = pltpu.make_async_copy(query_hbm.at[0], query_buf, load_sem.at[1])
    value_load = pltpu.make_async_copy(value_hbm.at[0], value_buf.at[rows_of(me)], load_sem.at[2])
    key_load.start()
    query_load.start()
    value_load.start()

    barrier = pltpu.get_barrier_semaphore()
    for off in range(1, n):
        pl.semaphore_signal(
            barrier, inc=1, device_id={"seq": lax.rem(me + off, n)}, device_id_type=MESH
        )
    pl.semaphore_wait(barrier, n - 1)

    def value_send(off, group):
        place = (rows_of(me), columns_of(group))
        return pltpu.make_async_remote_copy(
            src_ref=value_hbm.at[0, :, columns_of(group)],
            dst_ref=value_buf.at[place],
            send_sem=send_sem.at[off - 1, 0, group],
            recv_sem=recv_sem.at[off - 1, 0, group],
            device_id={"seq": lax.rem(me + off, n)},
            device_id_type=MESH,
        )

    def key_send(off, group):
        place = (rows_of(me), columns_of(group))
        return pltpu.make_async_remote_copy(
            src_ref=key_buf.at[place],
            dst_ref=key_buf.at[place],
            send_sem=send_sem.at[off - 1, 1, group],
            recv_sem=recv_sem.at[off - 1, 1, group],
            device_id={"seq": lax.rem(me + off, n)},
            device_id_type=MESH,
        )

    def arrival(buf, kind, off, group):
        place = (rows_of(lax.rem(me + n - off, n)), columns_of(group))
        return pltpu.make_async_remote_copy(
            src_ref=buf.at[place],
            dst_ref=buf.at[place],
            send_sem=send_sem.at[off - 1, kind, group],
            recv_sem=recv_sem.at[off - 1, kind, group],
            device_id={"seq": lax.rem(me + off, n)},
            device_id_type=MESH,
        )

    for group in range(min(AHEAD, groups)):
        for off in range(1, n):
            value_send(off, group).start()

    codes[me] = jnp.zeros(codes.shape[1:], jnp.int32)
    for b in range(block_count):
        used = counts[b, pl.ds(clip, 1), :]
        code = jnp.zeros((1, own_heads), jnp.int32)
        for s in range(block_count):
            named = lists[b, s, pl.ds(clip, 1), :]
            for e in range(block_count):
                code = code + jnp.where((named == e) & (used > s), 1 << e, 0)
        codes[me, pl.ds(b, 1), pl.ds(0, own_heads)] = code

    def code_send(off):
        return pltpu.make_async_remote_copy(
            src_ref=codes.at[me],
            dst_ref=codes.at[me],
            send_sem=code_send_sem.at[off - 1],
            recv_sem=code_recv_sem.at[off - 1],
            device_id={"seq": lax.rem(me + off, n)},
            device_id_type=MESH,
        )

    for off in range(1, n):
        code_send(off).start()

    def normalise(buf, first, gain):
        def step(i, carry):
            rows = pl.ds(pl.multiple_of(first + i * NORM_ROWS, NORM_ROWS), NORM_ROWS)
            values = buf[rows, :].astype(jnp.float32)
            spread = jnp.sum(values * values, axis=-1, keepdims=True) * (1.0 / width)
            buf[rows, :] = (values * lax.rsqrt(spread + EPSILON) * gain[...]).astype(jnp.bfloat16)
            return carry

        lax.fori_loop(0, tokens // NORM_ROWS, step, 0)

    key_load.wait()
    normalise(key_buf, me * tokens, key_gain)
    for group in range(min(AHEAD, groups)):
        for off in range(1, n):
            key_send(off, group).start()
    query_load.wait()
    normalise(query_buf, 0, query_gain)
    value_load.wait()
    for off in range(1, n):
        source = lax.rem(me + n - off, n)
        pltpu.make_async_remote_copy(
            src_ref=codes.at[source],
            dst_ref=codes.at[source],
            send_sem=code_send_sem.at[off - 1],
            recv_sem=code_recv_sem.at[off - 1],
            device_id={"seq": lax.rem(me + off, n)},
            device_id_type=MESH,
        ).wait_recv()
    code_load = pltpu.make_async_copy(codes, codes_smem, code_load_sem)
    code_load.start()
    code_load.wait()

    exponent_scale = math.log2(math.e) / math.sqrt(HD)

    def attend(head):
        columns = pl.ds(pl.multiple_of(head * HD, HD), HD)
        scores = lax.dot_general(
            query_buf[:, columns],
            key_buf[:, columns],
            (((1,), (1,)), ((), ())),
            preferred_element_type=jnp.float32,
        )
        owner = head // own_heads
        own_head = head - owner * own_heads
        weights, sums = [], []
        for r in range(tokens // row_group):
            code = codes_smem[owner, (me * tokens + r * row_group) // BLK, own_head]
            pieces = []
            for e in range(block_count):
                allowed = jnp.bitwise_and(code, 1 << e) != 0
                bias = jnp.where(allowed, jnp.float32(0.0), jnp.float32(MASKED))
                pieces.append(
                    scores[r * row_group : (r + 1) * row_group, e * BLK : (e + 1) * BLK] + bias
                )
            masked = jnp.concatenate(pieces, axis=1)
            highest = jnp.max(masked, axis=-1, keepdims=True)
            weight = jnp.exp2((masked - highest) * exponent_scale)
            sums.append(jnp.sum(weight, axis=-1, keepdims=True))
            weights.append(weight.astype(jnp.bfloat16))
        numerator = jnp.dot(
            jnp.concatenate(weights, axis=0),
            value_buf[:, columns],
            preferred_element_type=jnp.float32,
        )
        out_buf[:, columns] = (numerator / jnp.concatenate(sums, axis=0)).astype(jnp.bfloat16)

    def out_copy(group):
        return pltpu.make_async_copy(
            out_buf.at[:, columns_of(group)], out_hbm.at[0, :, columns_of(group)], out_sem.at[group]
        )

    def visit(group, carry):
        for off in range(1, n):
            value_send(off, group).wait_send()
            key_send(off, group).wait_send()

        @pl.when(group + AHEAD < groups)
        def _():
            for off in range(1, n):
                value_send(off, group + AHEAD).start()
                key_send(off, group + AHEAD).start()

        for off in range(1, n):
            arrival(value_buf, 0, off, group).wait_recv()
            arrival(key_buf, 1, off, group).wait_recv()
        for j in range(PAIR):
            attend(group * PAIR + j)
        out_copy(group).start()
        return carry

    lax.fori_loop(0, groups, visit, 0)

    def finish(group, carry):
        out_copy(group).wait()
        return carry

    lax.fori_loop(0, groups, finish, 0)
    for off in range(1, n):
        code_send(off).wait_send()


def shards(n, query_rows, key_rows, value_rows, query_gain, key_gain, tile_lists, tile_counts):
    _, tokens, width = query_rows.shape
    block_count = tile_lists.shape[2]
    groups = width // (PAIR * HD)
    code_rows = -(-block_count // 8) * 8
    buffers = (2 * n + 2) * tokens * width * 2
    in_hbm = pl.BlockSpec(memory_space=pl.ANY)
    in_vmem = pl.BlockSpec(memory_space=pltpu.VMEM)
    visited = tokens * n * tokens * width
    return pl.pallas_call(
        functools.partial(kernel, n),
        out_shape=jax.ShapeDtypeStruct(query_rows.shape, jnp.bfloat16),
        in_specs=[in_hbm] * 3 + [in_vmem] * 4,
        out_specs=in_hbm,
        scratch_shapes=[
            pltpu.VMEM((tokens, width), jnp.bfloat16),
            pltpu.VMEM((n * tokens, width), jnp.bfloat16),
            pltpu.VMEM((n * tokens, width), jnp.bfloat16),
            pltpu.VMEM((tokens, width), jnp.bfloat16),
            pltpu.VMEM((n, code_rows, 128), jnp.int32),
            pltpu.SMEM((n, code_rows, 128), jnp.int32),
            pltpu.SemaphoreType.DMA((3,)),
            pltpu.SemaphoreType.DMA((n - 1, 2, groups)),
            pltpu.SemaphoreType.DMA((n - 1, 2, groups)),
            pltpu.SemaphoreType.DMA((n - 1,)),
            pltpu.SemaphoreType.DMA((n - 1,)),
            pltpu.SemaphoreType.DMA,
            pltpu.SemaphoreType.DMA((groups,)),
        ],
        compiler_params=pltpu.CompilerParams(
            collective_id=0,
            has_side_effects=True,
            vmem_limit_bytes=buffers + 12 * 1024 * 1024,
        ),
        cost_estimate=pl.CostEstimate(
            flops=4 * visited, bytes_accessed=8 * tokens * width, transcendentals=visited // HD
        ),
    )(
        query_rows,
        key_rows,
        value_rows,
        query_gain.reshape(1, width),
        key_gain.reshape(1, width),
        jnp.transpose(tile_lists, (2, 3, 0, 1)),
        jnp.transpose(tile_counts, (2, 0, 1)),
    )


def solution(mesh):
    in_specs = (
        P("clip", "seq", None),
        P("clip", "seq", None),
        P("clip", "seq", None),
        P(),
        P(),
        P(None, "seq", None, None),
        P(None, "seq", None),
    )
    out_specs = P("clip", "seq", None)
    return jax.shard_map(
        functools.partial(shards, mesh.shape["seq"]),
        mesh=mesh,
        in_specs=in_specs,
        out_specs=out_specs,
        check_vma=False,
    )
```

profile of v0, /device:TPU:0, one launch (start us, length us, event | category | flops | bytes accessed | tf_op | source)
XLA Modules:
  0.0 99.8 jit_solution(7470078365614321363)
XLA Ops:
  0.0 0.0 copy-start
  0.0 1.5 %copy-done = bf16[1,192,5120]{2,1,0:T(8,128)(2,1)S(1)} copy-done((bf16[1,192,5120]{2,1,0:T(8,128)(2,1)S(1)}, bf16[1,192,5120]{2,1,0:T(8,128)(2,1)}, u32[]{:S(2)}) %copy-start) | copy-done | bytes 1966104
  1.5 0.0 copy-start.1
  1.5 1.5 %copy-done.1 = bf16[1,192,5120]{2,1,0:T(8,128)(2,1)S(1)} copy-done((bf16[1,192,5120]{2,1,0:T(8,128)(2,1)S(1)}, bf16[1,192,5120]{2,1,0:T(8,128)(2,1)}, u32[]{:S(2)}) %copy-start.1) | copy-done | bytes 1966104
  3.1 0.0 copy-start.2
  3.1 1.5 %copy-done.2 = bf16[1,192,5120]{2,1,0:T(8,128)(2,1)S(1)} copy-done((bf16[1,192,5120]{2,1,0:T(8,128)(2,1)S(1)}, bf16[1,192,5120]{2,1,0:T(8,128)(2,1)}, u32[]{:S(2)}) %copy-start.2) | copy-done | bytes 1966104
  4.6 0.0 copy-start.3
  4.6 0.9 copy-done.3
  5.5 0.0 copy-start.4
  5.5 0.7 copy-done.4
  6.3 0.0 copy-start.5
  6.3 0.7 copy-done.5
  7.0 0.0 copy-start.6
  7.0 0.7 copy-done.6
  7.7 90.8 %shard_map.73 = bf16[1,192,5120]{2,1,0:T(8,128)(2,1)S(1)} custom-call(bf16[1,192,5120]{2,1,0:T(8,128)(2,1)S(1)} %copy-done, bf16[1,192,5120]{2,1,0:T(8,128)(2,1)S(1)} %copy-done.1, bf16[1,192,5120]{2,1,0:T(8,128)(2,1)S(1)} %copy-done.2, f32[1,5120]{1,0:T(1,128)S(1)} %bitcast.6, f32[1,5120]{1,0:T(1,128)S(1)} %bitcast.7, s32[3,3,16,20]{3,2,1,0:T(8,128)S(1)} %bitcast.4, ...), custom_call_target="tpu_custom_call" | custom-call | flops 1509949440 | bytes 7864320 | tf_op jit(solution)/shard_map/pallas_call | solution.py:246
  98.5 1.3 %copy.9 = bf16[1,192,5120]{2,1,0:T(8,128)(2,1)} copy(bf16[1,192,5120]{2,1,0:T(8,128)(2,1)S(1)} %shard_map.73) | data formatting | bytes 3932160
Async XLA Ops:
  0.0 1.5 %copy-start = (bf16[1,192,5120]{2,1,0:T(8,128)(2,1)S(1)}, bf16[1,192,5120]{2,1,0:T(8,128)(2,1)}, u32[]{:S(2)}) copy-start(bf16[1,192,5120]{2,1,0:T(8,128)(2,1)} %query_hbm.1) | copy-start | bytes 5898244
  1.5 1.5 %copy-start.1 = (bf16[1,192,5120]{2,1,0:T(8,128)(2,1)S(1)}, bf16[1,192,5120]{2,1,0:T(8,128)(2,1)}, u32[]{:S(2)}) copy-start(bf16[1,192,5120]{2,1,0:T(8,128)(2,1)} %key_hbm.1) | copy-start | bytes 5898244
  3.1 1.5 %copy-start.2 = (bf16[1,192,5120]{2,1,0:T(8,128)(2,1)S(1)}, bf16[1,192,5120]{2,1,0:T(8,128)(2,1)}, u32[]{:S(2)}) copy-start(bf16[1,192,5120]{2,1,0:T(8,128)(2,1)} %value_hbm.1) | copy-start | bytes 5898244
  4.6 0.9 copy-start.3
  5.5 0.7 copy-start.4
  6.3 0.7 copy-start.5
  7.0 0.7 copy-start.6
where the time goes:
time: 100 us; the launch traced here: 99.8 us
  Pallas kernels  90.8 us (91%)
  local copies, waits for them, and re-layouts  8.98 us (9%)
    pallas_call x1, Pallas kernels, shards(): pl.pallas_call(functools.partial(kernel, n), out_shape=jax.ShapeDtypeStru...  90.8 us
    unnamed x15, local copies, waits for them, and re-layouts  8.98 us

commit v1 on v0

v1 whole, which is shorter than its diff:
```python
import functools
import math

import jax
import jax.numpy as jnp
from jax import lax
from jax.experimental import pallas as pl
from jax.experimental.pallas import tpu as pltpu
from jax.sharding import PartitionSpec as P

HD = 128
BLK = 128
PAIR = 2
AHEAD = 3
NORM_ROWS = 16
MASKED = -1e30
VMEM_BYTES = 60 * 1024 * 1024
EPSILON = 1e-06

MESH = pl.DeviceIdType.MESH


def kernel(
    n,
    query_hbm,
    key_hbm,
    value_hbm,
    query_gain_hbm,
    key_gain_hbm,
    lists_hbm,
    counts_hbm,
    out_hbm,
    query_raw,
    key_raw,
    query_buf,
    key_buf,
    value_buf,
    out_buf,
    query_gain,
    key_gain,
    lists,
    counts,
    codes,
    codes_smem,
    load_sem,
    value_sem,
    send_sem,
    recv_sem,
    code_send_sem,
    code_recv_sem,
    code_load_sem,
    out_sem,
):
    tokens, width = query_raw.shape
    groups, _, group_width = key_buf.shape
    own_heads = lists.shape[3]
    block_count = lists.shape[0]
    row_group = math.gcd(tokens, BLK)
    first = min(AHEAD, groups)
    me = lax.axis_index("seq")
    clip = lax.axis_index("clip")

    def rows_of(device):
        return pl.ds(pl.multiple_of(device * tokens, row_group), tokens)

    def value_load(group):
        columns = pl.ds(pl.multiple_of(group * group_width, group_width), group_width)
        return pltpu.make_async_copy(
            value_hbm.at[0, :, columns], value_buf.at[group, rows_of(me)], value_sem.at[group]
        )

    loads = [
        pltpu.make_async_copy(source, target, load_sem.at[i])
        for i, (source, target) in enumerate(
            [
                (key_hbm.at[0], key_raw),
                (key_gain_hbm, key_gain),
                (lists_hbm, lists),
                (counts_hbm, counts),
                (query_hbm.at[0], query_raw),
                (query_gain_hbm, query_gain),
            ]
        )
    ]
    for group in range(first):
        value_load(group).start()
    for load in loads:
        load.start()

    barrier = pltpu.get_barrier_semaphore()
    for off in range(1, n):
        pl.semaphore_signal(
            barrier, inc=1, device_id={"seq": lax.rem(me + off, n)}, device_id_type=MESH
        )

    def load_values(group, carry):
        value_load(group).start()
        return carry

    lax.fori_loop(first, groups, load_values, 0)
    pl.semaphore_wait(barrier, n - 1)

    def message(buf, kind, off, group, source):
        place = (group, rows_of(source))
        return pltpu.make_async_remote_copy(
            src_ref=buf.at[place],
            dst_ref=buf.at[place],
            send_sem=send_sem.at[off - 1, kind, group],
            recv_sem=recv_sem.at[off - 1, kind, group],
            device_id={"seq": lax.rem(me + off, n)},
            device_id_type=MESH,
        )

    def value_send(off, group):
        return message(value_buf, 0, off, group, me)

    def key_send(off, group):
        return message(key_buf, 1, off, group, me)

    for group in range(first):
        value_load(group).wait()
        for off in range(1, n):
            value_send(off, group).start()

    def normalise(raw, gain, target, first_row):
        def step(i, carry):
            rows = pl.ds(pl.multiple_of(i * NORM_ROWS, NORM_ROWS), NORM_ROWS)
            rows_to = pl.ds(pl.multiple_of(first_row + i * NORM_ROWS, NORM_ROWS), NORM_ROWS)
            total = jnp.zeros((NORM_ROWS, group_width), jnp.float32)
            for g in range(groups):
                part = raw[rows, g * group_width : (g + 1) * group_width].astype(jnp.float32)
                total = total + part * part
            spread = jnp.sum(total, axis=-1, keepdims=True) * (1.0 / width)
            factor = lax.rsqrt(spread + EPSILON)
            for g in range(groups):
                columns = slice(g * group_width, (g + 1) * group_width)
                part = raw[rows, columns].astype(jnp.float32)
                target[g, rows_to, :] = (part * factor * gain[:, columns]).astype(jnp.bfloat16)
            return carry

        lax.fori_loop(0, tokens // NORM_ROWS, step, 0)

    loads[0].wait()
    loads[1].wait()
    normalise(key_raw, key_gain, key_buf, me * tokens)
    for group in range(first):
        for off in range(1, n):
            key_send(off, group).start()

    loads[2].wait()
    loads[3].wait()
    codes[me] = jnp.zeros(codes.shape[1:], jnp.int32)
    for b in range(block_count):
        used = counts[b, pl.ds(clip, 1), :]
        code = jnp.zeros((1, own_heads), jnp.int32)
        for s in range(block_count):
            named = lists[b, s, pl.ds(clip, 1), :]
            for e in range(block_count):
                code = code + jnp.where((named == e) & (used > s), 1 << e, 0)
        codes[me, pl.ds(b, 1), pl.ds(0, own_heads)] = code

    def code_message(off, source):
        return pltpu.make_async_remote_copy(
            src_ref=codes.at[source],
            dst_ref=codes.at[source],
            send_sem=code_send_sem.at[off - 1],
            recv_sem=code_recv_sem.at[off - 1],
            device_id={"seq": lax.rem(me + off, n)},
            device_id_type=MESH,
        )

    for off in range(1, n):
        code_message(off, me).start()
    loads[4].wait()
    loads[5].wait()
    normalise(query_raw, query_gain, query_buf, 0)
    for off in range(1, n):
        code_message(off, lax.rem(me + n - off, n)).wait_recv()
    code_load = pltpu.make_async_copy(codes, codes_smem, code_load_sem)
    code_load.start()
    code_load.wait()

    exponent_scale = math.log2(math.e) / math.sqrt(HD)

    def attend(group, j):
        head = group * PAIR + j
        columns = slice(j * HD, (j + 1) * HD)
        scores = lax.dot_general(
            query_buf[group, :, columns],
            key_buf[group, :, columns],
            (((1,), (1,)), ((), ())),
            preferred_element_type=jnp.float32,
        )
        owner = head // own_heads
        own_head = head - owner * own_heads
        weights, sums = [], []
        for r in range(tokens // row_group):
            code = codes_smem[owner, (me * tokens + r * row_group) // BLK, own_head]
            pieces = []
            for e in range(block_count):
                allowed = jnp.bitwise_and(code, 1 << e) != 0
                bias = jnp.where(allowed, jnp.float32(0.0), jnp.float32(MASKED))
                pieces.append(
                    scores[r * row_group : (r + 1) * row_group, e * BLK : (e + 1) * BLK] + bias
                )
            masked = jnp.concatenate(pieces, axis=1)
            highest = jnp.max(masked, axis=-1, keepdims=True)
            weight = jnp.exp2((masked - highest) * exponent_scale)
            sums.append(jnp.sum(weight, axis=-1, keepdims=True))
            weights.append(weight.astype(jnp.bfloat16))
        numerator = jnp.dot(
            jnp.concatenate(weights, axis=0),
            value_buf[group, :, columns],
            preferred_element_type=jnp.float32,
        )
        out_buf[:, pl.ds(pl.multiple_of(head * HD, HD), HD)] = (
            numerator / jnp.concatenate(sums, axis=0)
        ).astype(jnp.bfloat16)

    def out_copy(group):
        columns = pl.ds(pl.multiple_of(group * group_width, group_width), group_width)
        return pltpu.make_async_copy(
            out_buf.at[:, columns], out_hbm.at[0, :, columns], out_sem.at[group]
        )

    def visit(group, carry):
        for off in range(1, n):
            value_send(off, group).wait_send()
            key_send(off, group).wait_send()

        @pl.when(group + AHEAD < groups)
        def _():
            value_load(group + AHEAD).wait()
            for off in range(1, n):
                value_send(off, group + AHEAD).start()
                key_send(off, group + AHEAD).start()

        for off in range(1, n):
            source = lax.rem(me + n - off, n)
            message(value_buf, 0, off, group, source).wait_recv()
            message(key_buf, 1, off, group, source).wait_recv()
        for j in range(PAIR):
            attend(group, j)
        out_copy(group).start()
        return carry

    lax.fori_loop(0, groups, visit, 0)

    def finish(group, carry):
        out_copy(group).wait()
        return carry

    lax.fori_loop(0, groups, finish, 0)
    for off in range(1, n):
        code_message(off, me).wait_send()


def shards(n, query_rows, key_rows, value_rows, query_gain, key_gain, tile_lists, tile_counts):
    _, tokens, width = query_rows.shape
    lists = jnp.transpose(tile_lists, (2, 3, 0, 1))
    counts = jnp.transpose(tile_counts, (2, 0, 1))
    block_count = lists.shape[0]
    group_width = PAIR * HD
    groups = width // group_width
    code_rows = -(-block_count // 8) * 8
    visited = tokens * n * tokens * width
    return pl.pallas_call(
        functools.partial(kernel, n),
        out_shape=jax.ShapeDtypeStruct(query_rows.shape, jnp.bfloat16),
        in_specs=[pl.BlockSpec(memory_space=pltpu.HBM)] * 7,
        out_specs=pl.BlockSpec(memory_space=pltpu.HBM),
        scratch_shapes=[
            pltpu.VMEM((tokens, width), jnp.bfloat16),
            pltpu.VMEM((tokens, width), jnp.bfloat16),
            pltpu.VMEM((groups, tokens, group_width), jnp.bfloat16),
            pltpu.VMEM((groups, n * tokens, group_width), jnp.bfloat16),
            pltpu.VMEM((groups, n * tokens, group_width), jnp.bfloat16),
            pltpu.VMEM((tokens, width), jnp.bfloat16),
            pltpu.VMEM((1, width), jnp.float32),
            pltpu.VMEM((1, width), jnp.float32),
            pltpu.VMEM(lists.shape, jnp.int32),
            pltpu.VMEM(counts.shape, jnp.int32),
            pltpu.VMEM((n, code_rows, 128), jnp.int32),
            pltpu.SMEM((n, code_rows, 128), jnp.int32),
            pltpu.SemaphoreType.DMA((6,)),
            pltpu.SemaphoreType.DMA((groups,)),
            pltpu.SemaphoreType.DMA((n - 1, 2, groups)),
            pltpu.SemaphoreType.DMA((n - 1, 2, groups)),
            pltpu.SemaphoreType.DMA((n - 1,)),
            pltpu.SemaphoreType.DMA((n - 1,)),
            pltpu.SemaphoreType.DMA,
            pltpu.SemaphoreType.DMA((groups,)),
        ],
        compiler_params=pltpu.CompilerParams(
            collective_id=0,
            has_side_effects=True,
            vmem_limit_bytes=VMEM_BYTES,
        ),
        cost_estimate=pl.CostEstimate(
            flops=4 * visited, bytes_accessed=8 * tokens * width, transcendentals=visited // HD
        ),
    )(
        query_rows,
        key_rows,
        value_rows,
        query_gain.reshape(1, width),
        key_gain.reshape(1, width),
        lists,
        counts,
    )


def solution(mesh):
    in_specs = (
        P("clip", "seq", None),
        P("clip", "seq", None),
        P("clip", "seq", None),
        P(),
        P(),
        P(None, "seq", None, None),
        P(None, "seq", None),
    )
    out_specs = P("clip", "seq", None)
    return jax.shard_map(
        functools.partial(shards, mesh.shape["seq"]),
        mesh=mesh,
        in_specs=in_specs,
        out_specs=out_specs,
        check_vma=False,
    )
```

time: 100 us -> 95.9 us (0.959)
  local copies, waits for them, and re-layouts: 8.98 us -> 2.94 us
  Pallas kernels: 90.8 us -> 92.8 us
    unnamed x15 -> x1, local copies, waits for them, and re-layouts: 8.98 us -> 2.94 us
    pallas_call x1, Pallas kernels: 90.8 us -> 92.8 us  [shards(): pl.pallas_call(functools.partial(kernel, n), out_shape=jax.ShapeDtypeStru...]
where the time goes in v1:
time: 95.9 us; the launch traced here: 95.8 us
  Pallas kernels  92.8 us (97%)
  local copies, waits for them, and re-layouts  2.94 us (3%)
    pallas_call x1, Pallas kernels, shards(): pl.pallas_call(functools.partial(kernel, n), out_shape=jax.ShapeDtypeStru...  92.8 us
    unnamed x1, local copies, waits for them, and re-layouts  2.94 us

profile of v1, /device:TPU:0, one launch (start us, length us, event | category | flops | bytes accessed | tf_op | source)
XLA Modules:
  0.0 95.8 jit_solution(11657499631838788122)
XLA Ops:
  0.0 92.8 %shard_map.73 = bf16[1,192,5120]{2,1,0:T(8,128)(2,1)} custom-call(bf16[1,192,5120]{2,1,0:T(8,128)(2,1)} %query_hbm.1, bf16[1,192,5120]{2,1,0:T(8,128)(2,1)} %key_hbm.1, bf16[1,192,5120]{2,1,0:T(8,128)(2,1)} %value_hbm.1, f32[1,5120]{1,0:T(1,128)} %bitcast.6, f32[1,5120]{1,0:T(1,128)} %bitcast.7, s32[3,3,16,20]{3,2,1,0:T(8,128)} %bitcast.4, s32[3,16,20]{2,1,0:T(8,128)} %bitcast.5), custom_call_target="tpu_custom_call" | custom-call | flops 1509949440 | bytes 7864320 | tf_op jit(solution)/shard_map/pallas_call | solution.py:267
  92.9 2.9 %copy.9 = bf16[1,192,5120]{2,1,0:T(8,128)(2,1)} copy(bf16[1,192,5120]{2,1,0:T(8,128)(2,1)} %shard_map.73) | data formatting | bytes 3932160

commit v2 on v1

--- a/solution.py
+++ b/solution.py
@@ -14,7 +14,7 @@
 AHEAD = 3
 NORM_ROWS = 16
 MASKED = -1e30
-VMEM_BYTES = 60 * 1024 * 1024
+VMEM_BYTES = 48 * 1024 * 1024
 EPSILON = 1e-06
 
 MESH = pl.DeviceIdType.MESH
@@ -29,13 +29,12 @@
     key_gain_hbm,
     lists_hbm,
     counts_hbm,
-    out_hbm,
+    out_ref,
     query_raw,
     key_raw,
     query_buf,
     key_buf,
     value_buf,
-    out_buf,
     query_gain,
     key_gain,
     lists,
@@ -49,7 +48,6 @@
     code_send_sem,
     code_recv_sem,
     code_load_sem,
-    out_sem,
 ):
     tokens, width = query_raw.shape
     groups, _, group_width = key_buf.shape
@@ -182,7 +180,7 @@
 
     exponent_scale = math.log2(math.e) / math.sqrt(HD)
 
-    def attend(group, j):
+    def weigh(group, j):
         head = group * PAIR + j
         columns = slice(j * HD, (j + 1) * HD)
         scores = lax.dot_general(
@@ -208,20 +206,16 @@
             weight = jnp.exp2((masked - highest) * exponent_scale)
             sums.append(jnp.sum(weight, axis=-1, keepdims=True))
             weights.append(weight.astype(jnp.bfloat16))
+        return jnp.concatenate(weights, axis=0), 1.0 / jnp.concatenate(sums, axis=0)
+
+    def gather(group, j, weight, inverse):
         numerator = jnp.dot(
-            jnp.concatenate(weights, axis=0),
-            value_buf[group, :, columns],
+            weight,
+            value_buf[group, :, j * HD : (j + 1) * HD],
             preferred_element_type=jnp.float32,
         )
-        out_buf[:, pl.ds(pl.multiple_of(head * HD, HD), HD)] = (
-            numerator / jnp.concatenate(sums, axis=0)
-        ).astype(jnp.bfloat16)
-
-    def out_copy(group):
-        columns = pl.ds(pl.multiple_of(group * group_width, group_width), group_width)
-        return pltpu.make_async_copy(
-            out_buf.at[:, columns], out_hbm.at[0, :, columns], out_sem.at[group]
-        )
+        columns = pl.ds(pl.multiple_of((group * PAIR + j) * HD, HD), HD)
+        out_ref[0, :, columns] = (numerator * inverse).astype(jnp.bfloat16)
 
     def visit(group, carry):
         for off in range(1, n):
@@ -232,25 +226,21 @@
         def _():
             value_load(group + AHEAD).wait()
             for off in range(1, n):
+                key_send(off, group + AHEAD).start()
+            for off in range(1, n):
                 value_send(off, group + AHEAD).start()
-                key_send(off, group + AHEAD).start()
-
-        for off in range(1, n):
-            source = lax.rem(me + n - off, n)
+
+        sources = [(off, lax.rem(me + n - off, n)) for off in range(1, n)]
+        for off, source in sources:
+            message(key_buf, 1, off, group, source).wait_recv()
+        weighed = [weigh(group, j) for j in range(PAIR)]
+        for off, source in sources:
             message(value_buf, 0, off, group, source).wait_recv()
-            message(key_buf, 1, off, group, source).wait_recv()
         for j in range(PAIR):
-            attend(group, j)
-        out_copy(group).start()
+            gather(group, j, *weighed[j])
         return carry
 
     lax.fori_loop(0, groups, visit, 0)
-
-    def finish(group, carry):
-        out_copy(group).wait()
-        return carry
-
-    lax.fori_loop(0, groups, finish, 0)
     for off in range(1, n):
         code_message(off, me).wait_send()
 
@@ -266,16 +256,15 @@
     visited = tokens * n * tokens * width
     return pl.pallas_call(
         functools.partial(kernel, n),
-        out_shape=jax.ShapeDtypeStruct(query_rows.shape, jnp.bfloat16),
+        out_shape=pltpu.VMEM(query_rows.shape, jnp.bfloat16),
         in_specs=[pl.BlockSpec(memory_space=pltpu.HBM)] * 7,
-        out_specs=pl.BlockSpec(memory_space=pltpu.HBM),
+        out_specs=pl.BlockSpec(memory_space=pltpu.VMEM),
         scratch_shapes=[
             pltpu.VMEM((tokens, width), jnp.bfloat16),
             pltpu.VMEM((tokens, width), jnp.bfloat16),
             pltpu.VMEM((groups, tokens, group_width), jnp.bfloat16),
             pltpu.VMEM((groups, n * tokens, group_width), jnp.bfloat16),
             pltpu.VMEM((groups, n * tokens, group_width), jnp.bfloat16),
-            pltpu.VMEM((tokens, width), jnp.bfloat16),
             pltpu.VMEM((1, width), jnp.float32),
             pltpu.VMEM((1, width), jnp.float32),
             pltpu.VMEM(lists.shape, jnp.int32),
@@ -289,7 +278,6 @@
             pltpu.SemaphoreType.DMA((n - 1,)),
             pltpu.SemaphoreType.DMA((n - 1,)),
             pltpu.SemaphoreType.DMA,
-            pltpu.SemaphoreType.DMA((groups,)),
         ],
         compiler_params=pltpu.CompilerParams(
             collective_id=0,
@@ -300,13 +288,18 @@
             flops=4 * visited, bytes_accessed=8 * tokens * width, transcendentals=visited // HD
         ),
     )(
-        query_rows,
-        key_rows,
-        value_rows,
-        query_gain.reshape(1, width),
-        key_gain.reshape(1, width),
-        lists,
-        counts,
+        *(
+            pltpu.with_memory_space_constraint(operand, pltpu.HBM)
+            for operand in (
+                query_rows,
+                key_rows,
+                value_rows,
+                query_gain.reshape(1, width),
+                key_gain.reshape(1, width),
+                lists,
+                counts,
+            )
+        )
     )
 
 

time: 95.9 us -> 92.9 us (0.969)
  local copies, waits for them, and re-layouts: 2.94 us -> 1.27 us
  Pallas kernels: 92.8 us -> 91.5 us
    unnamed x1, local copies, waits for them, and re-layouts: 2.94 us -> 1.27 us
    pallas_call x1, Pallas kernels: 92.8 us -> 91.5 us  [shards(): pl.pallas_call(functools.partial(kernel, n), out_shape=pltpu.VMEM(query_r...]
where the time goes in v2:
time: 92.9 us; the launch traced here: 92.8 us
  Pallas kernels  91.5 us (98%)
  local copies, waits for them, and re-layouts  1.27 us (1%)
    pallas_call x1, Pallas kernels, shards(): pl.pallas_call(functools.partial(kernel, n), out_shape=pltpu.VMEM(query_r...  91.5 us

profile of v2, /device:TPU:0, one launch (start us, length us, event | category | flops | bytes accessed | tf_op | source)
XLA Modules:
  0.0 92.8 jit_solution(15479474427651381590)
XLA Ops:
  0.0 91.5 %shard_map.73 = bf16[1,192,5120]{2,1,0:T(8,128)(2,1)S(1)} custom-call(bf16[1,192,5120]{2,1,0:T(8,128)(2,1)} %query_hbm.1, bf16[1,192,5120]{2,1,0:T(8,128)(2,1)} %key_hbm.1, bf16[1,192,5120]{2,1,0:T(8,128)(2,1)} %value_hbm.1, f32[1,5120]{1,0:T(1,128)} %bitcast.6, f32[1,5120]{1,0:T(1,128)} %bitcast.7, s32[3,3,16,20]{3,2,1,0:T(8,128)} %bitcast.4, ...), custom_call_target="tpu_custom_call" | custom-call | flops 1509949440 | bytes 7864320 | tf_op jit(solution)/shard_map/pallas_call | solution.py:257
  91.5 1.3 %copy.9 = bf16[1,192,5120]{2,1,0:T(8,128)(2,1)} copy(bf16[1,192,5120]{2,1,0:T(8,128)(2,1)S(1)} %shard_map.73) | data formatting | bytes 3932160

commit v3 on v2

--- a/solution.py
+++ b/solution.py
@@ -11,7 +11,7 @@
 HD = 128
 BLK = 128
 PAIR = 2
-AHEAD = 3
+AHEAD = 8
 NORM_ROWS = 16
 MASKED = -1e30
 VMEM_BYTES = 48 * 1024 * 1024

time: 92.9 us -> 92.9 us (level)
  no operation moved by 1% of the time
where the time goes in v3:
time: 92.9 us; the launch traced here: 92.7 us
  Pallas kernels  91.4 us (98%)
  local copies, waits for them, and re-layouts  1.27 us (1%)
    pallas_call x1, Pallas kernels, shards(): pl.pallas_call(functools.partial(kernel, n), out_shape=pltpu.VMEM(query_r...  91.4 us

profile of v3, /device:TPU:0, one launch (start us, length us, event | category | flops | bytes accessed | tf_op | source)
XLA Modules:
  0.0 92.7 jit_solution(8278512040996983361)
XLA Ops:
  0.0 91.4 %shard_map.73 = bf16[1,192,5120]{2,1,0:T(8,128)(2,1)S(1)} custom-call(bf16[1,192,5120]{2,1,0:T(8,128)(2,1)} %query_hbm.1, bf16[1,192,5120]{2,1,0:T(8,128)(2,1)} %key_hbm.1, bf16[1,192,5120]{2,1,0:T(8,128)(2,1)} %value_hbm.1, f32[1,5120]{1,0:T(1,128)} %bitcast.6, f32[1,5120]{1,0:T(1,128)} %bitcast.7, s32[3,3,16,20]{3,2,1,0:T(8,128)} %bitcast.4, ...), custom_call_target="tpu_custom_call" | custom-call | flops 1509949440 | bytes 7864320 | tf_op jit(solution)/shard_map/pallas_call | solution.py:257
  91.5 1.3 %copy.9 = bf16[1,192,5120]{2,1,0:T(8,128)(2,1)} copy(bf16[1,192,5120]{2,1,0:T(8,128)(2,1)S(1)} %shard_map.73) | data formatting | bytes 3932160

commit v4 on v3

--- a/solution.py
+++ b/solution.py
@@ -11,7 +11,7 @@
 HD = 128
 BLK = 128
 PAIR = 2
-AHEAD = 8
+AHEAD = 4
 NORM_ROWS = 16
 MASKED = -1e30
 VMEM_BYTES = 48 * 1024 * 1024
@@ -80,22 +80,13 @@
             ]
         )
     ]
-    for group in range(first):
-        value_load(group).start()
-    for load in loads:
-        load.start()
-
     barrier = pltpu.get_barrier_semaphore()
     for off in range(1, n):
         pl.semaphore_signal(
             barrier, inc=1, device_id={"seq": lax.rem(me + off, n)}, device_id_type=MESH
         )
-
-    def load_values(group, carry):
-        value_load(group).start()
-        return carry
-
-    lax.fori_loop(first, groups, load_values, 0)
+    for load in loads:
+        load.start()
     pl.semaphore_wait(barrier, n - 1)
 
     def message(buf, kind, off, group, source):
@@ -110,15 +101,28 @@
         )
 
     def value_send(off, group):
-        return message(value_buf, 0, off, group, me)
+        columns = pl.ds(pl.multiple_of(group * group_width, group_width), group_width)
+        return pltpu.make_async_remote_copy(
+            src_ref=value_hbm.at[0, :, columns],
+            dst_ref=value_buf.at[group, rows_of(me)],
+            send_sem=send_sem.at[off - 1, 0, group],
+            recv_sem=recv_sem.at[off - 1, 0, group],
+            device_id={"seq": lax.rem(me + off, n)},
+            device_id_type=MESH,
+        )
 
     def key_send(off, group):
         return message(key_buf, 1, off, group, me)
 
     for group in range(first):
-        value_load(group).wait()
         for off in range(1, n):
             value_send(off, group).start()
+
+    def load_values(group, carry):
+        value_load(group).start()
+        return carry
+
+    lax.fori_loop(0, groups, load_values, 0)
 
     def normalise(raw, gain, target, first_row):
         def step(i, carry):
@@ -224,7 +228,6 @@
 
         @pl.when(group + AHEAD < groups)
         def _():
-            value_load(group + AHEAD).wait()
             for off in range(1, n):
                 key_send(off, group + AHEAD).start()
             for off in range(1, n):
@@ -234,6 +237,7 @@
         for off, source in sources:
             message(key_buf, 1, off, group, source).wait_recv()
         weighed = [weigh(group, j) for j in range(PAIR)]
+        value_load(group).wait()
         for off, source in sources:
             message(value_buf, 0, off, group, source).wait_recv()
         for j in range(PAIR):

time: 92.9 us -> 93.1 us (level)
  no operation moved by 1% of the time
where the time goes in v4:
time: 93.1 us; the launch traced here: 92.9 us
  Pallas kernels  91.6 us (98%)
  local copies, waits for them, and re-layouts  1.27 us (1%)
    pallas_call x1, Pallas kernels, shards(): pl.pallas_call(functools.partial(kernel, n), out_shape=pltpu.VMEM(query_r...  91.6 us

profile of v4, /device:TPU:0, one launch (start us, length us, event | category | flops | bytes accessed | tf_op | source)
XLA Modules:
  0.0 92.9 jit_solution(11376538358887230060)
XLA Ops:
  0.0 91.6 %shard_map.73 = bf16[1,192,5120]{2,1,0:T(8,128)(2,1)S(1)} custom-call(bf16[1,192,5120]{2,1,0:T(8,128)(2,1)} %query_hbm.1, bf16[1,192,5120]{2,1,0:T(8,128)(2,1)} %key_hbm.1, bf16[1,192,5120]{2,1,0:T(8,128)(2,1)} %value_hbm.1, f32[1,5120]{1,0:T(1,128)} %bitcast.6, f32[1,5120]{1,0:T(1,128)} %bitcast.7, s32[3,3,16,20]{3,2,1,0:T(8,128)} %bitcast.4, ...), custom_call_target="tpu_custom_call" | custom-call | flops 1509949440 | bytes 7864320 | tf_op jit(solution)/shard_map/pallas_call | solution.py:261
  91.6 1.3 %copy.9 = bf16[1,192,5120]{2,1,0:T(8,128)(2,1)} copy(bf16[1,192,5120]{2,1,0:T(8,128)(2,1)S(1)} %shard_map.73) | data formatting | bytes 3932160

commit v5 on v4

--- a/solution.py
+++ b/solution.py
@@ -10,8 +10,8 @@
 
 HD = 128
 BLK = 128
-PAIR = 2
-AHEAD = 4
+PAIR = 4
+AHEAD = 3
 NORM_ROWS = 16
 MASKED = -1e30
 VMEM_BYTES = 48 * 1024 * 1024

time: 93.1 us -> 92.7 us (level)
  no operation moved by 1% of the time
where the time goes in v5:
time: 92.7 us; the launch traced here: 92.5 us
  Pallas kernels  91.3 us (98%)
  local copies, waits for them, and re-layouts  1.27 us (1%)
    pallas_call x1, Pallas kernels, shards(): pl.pallas_call(functools.partial(kernel, n), out_shape=pltpu.VMEM(query_r...  91.3 us

profile of v5, /device:TPU:0, one launch (start us, length us, event | category | flops | bytes accessed | tf_op | source)
XLA Modules:
  0.0 92.5 jit_solution(8781655253244262734)
XLA Ops:
  0.0 91.3 %shard_map.73 = bf16[1,192,5120]{2,1,0:T(8,128)(2,1)S(1)} custom-call(bf16[1,192,5120]{2,1,0:T(8,128)(2,1)} %query_hbm.1, bf16[1,192,5120]{2,1,0:T(8,128)(2,1)} %key_hbm.1, bf16[1,192,5120]{2,1,0:T(8,128)(2,1)} %value_hbm.1, f32[1,5120]{1,0:T(1,128)} %bitcast.6, f32[1,5120]{1,0:T(1,128)} %bitcast.7, s32[3,3,16,20]{3,2,1,0:T(8,128)} %bitcast.4, ...), custom_call_target="tpu_custom_call" | custom-call | flops 1509949440 | bytes 7864320 | tf_op jit(solution)/shard_map/pallas_call | solution.py:261
  91.3 1.3 %copy.9 = bf16[1,192,5120]{2,1,0:T(8,128)(2,1)} copy(bf16[1,192,5120]{2,1,0:T(8,128)(2,1)S(1)} %shard_map.73) | data formatting | bytes 3932160

commit v6 on v4

--- a/solution.py
+++ b/solution.py
@@ -30,6 +30,7 @@
     lists_hbm,
     counts_hbm,
     out_ref,
+    value_far,
     query_raw,
     key_raw,
     query_buf,
@@ -48,6 +49,7 @@
     code_send_sem,
     code_recv_sem,
     code_load_sem,
+    fetch_sem,
 ):
     tokens, width = query_raw.shape
     groups, _, group_width = key_buf.shape
@@ -104,11 +106,31 @@
         columns = pl.ds(pl.multiple_of(group * group_width, group_width), group_width)
         return pltpu.make_async_remote_copy(
             src_ref=value_hbm.at[0, :, columns],
-            dst_ref=value_buf.at[group, rows_of(me)],
+            dst_ref=value_far.at[me, :, columns],
             send_sem=send_sem.at[off - 1, 0, group],
             recv_sem=recv_sem.at[off - 1, 0, group],
             device_id={"seq": lax.rem(me + off, n)},
             device_id_type=MESH,
+        )
+
+    def value_arrival(off, group, source):
+        columns = pl.ds(pl.multiple_of(group * group_width, group_width), group_width)
+        place = (source, slice(None), columns)
+        return pltpu.make_async_remote_copy(
+            src_ref=value_far.at[place],
+            dst_ref=value_far.at[place],
+            send_sem=send_sem.at[off - 1, 0, group],
+            recv_sem=recv_sem.at[off - 1, 0, group],
+            device_id={"seq": lax.rem(me + off, n)},
+            device_id_type=MESH,
+        )
+
+    def value_fetch(off, group, source):
+        columns = pl.ds(pl.multiple_of(group * group_width, group_width), group_width)
+        return pltpu.make_async_copy(
+            value_far.at[source, :, columns],
+            value_buf.at[group, rows_of(source)],
+            fetch_sem.at[off - 1, group],
         )
 
     def key_send(off, group):
@@ -239,7 +261,10 @@
         weighed = [weigh(group, j) for j in range(PAIR)]
         value_load(group).wait()
         for off, source in sources:
-            message(value_buf, 0, off, group, source).wait_recv()
+            value_arrival(off, group, source).wait_recv()
+            value_fetch(off, group, source).start()
+        for off, source in sources:
+            value_fetch(off, group, source).wait()
         for j in range(PAIR):
             gather(group, j, *weighed[j])
         return carry
@@ -258,11 +283,17 @@
     groups = width // group_width
     code_rows = -(-block_count // 8) * 8
     visited = tokens * n * tokens * width
-    return pl.pallas_call(
+    attended, _ = pl.pallas_call(
         functools.partial(kernel, n),
-        out_shape=pltpu.VMEM(query_rows.shape, jnp.bfloat16),
+        out_shape=(
+            pltpu.VMEM(query_rows.shape, jnp.bfloat16),
+            pltpu.HBM((n, tokens, width), jnp.bfloat16),
+        ),
         in_specs=[pl.BlockSpec(memory_space=pltpu.HBM)] * 7,
-        out_specs=pl.BlockSpec(memory_space=pltpu.VMEM),
+        out_specs=(
+            pl.BlockSpec(memory_space=pltpu.VMEM),
+            pl.BlockSpec(memory_space=pltpu.HBM),
+        ),
         scratch_shapes=[
             pltpu.VMEM((tokens, width), jnp.bfloat16),
             pltpu.VMEM((tokens, width), jnp.bfloat16),
@@ -282,6 +313,7 @@
             pltpu.SemaphoreType.DMA((n - 1,)),
             pltpu.SemaphoreType.DMA((n - 1,)),
             pltpu.SemaphoreType.DMA,
+            pltpu.SemaphoreType.DMA((n - 1, groups)),
         ],
         compiler_params=pltpu.CompilerParams(
             collective_id=0,
@@ -305,6 +337,7 @@
             )
         )
     )
+    return attended
 
 
 def solution(mesh):

time: 93.1 us -> 94.8 us (1.018)
  Pallas kernels: 91.6 us -> 92.8 us
    pallas_call x1, Pallas kernels: 91.6 us -> 92.8 us  [shards(): pl.pallas_call(functools.partial(kernel, n), out_shape=(pltpu.VMEM(query_...]
where the time goes in v6:
time: 94.8 us; the launch traced here: 94.1 us
  Pallas kernels  92.8 us (98%)
  local copies, waits for them, and re-layouts  1.27 us (1%)
    pallas_call x1, Pallas kernels, shards(): pl.pallas_call(functools.partial(kernel, n), out_shape=(pltpu.VMEM(query_...  92.8 us

profile of v6, /device:TPU:0, one launch (start us, length us, event | category | flops | bytes accessed | tf_op | source)
XLA Modules:
  0.0 94.1 jit_solution(14356724457230114741)
XLA Ops:
  0.0 92.8 %shard_map.73 = (bf16[1,192,5120]{2,1,0:T(8,128)(2,1)S(1)}, bf16[2,192,5120]{2,1,0:T(8,128)(2,1)}) custom-call(bf16[1,192,5120]{2,1,0:T(8,128)(2,1)} %query_hbm.1, bf16[1,192,5120]{2,1,0:T(8,128)(2,1)} %key_hbm.1, bf16[1,192,5120]{2,1,0:T(8,128)(2,1)} %value_hbm.1, f32[1,5120]{1,0:T(1,128)} %bitcast.6, f32[1,5120]{1,0:T(1,128)} %bitcast.7, ...), custom_call_target="tpu_custom_call" | custom-call | flops 1509949440 | bytes 7864320 | tf_op jit(solution)/shard_map/pallas_call | solution.py:286
  92.8 1.3 %copy.9 = bf16[1,192,5120]{2,1,0:T(8,128)(2,1)} copy(bf16[1,192,5120]{2,1,0:T(8,128)(2,1)S(1)} %get-tuple-element.6) | data formatting | bytes 3932160

commit v7 on v5

--- a/solution.py
+++ b/solution.py
@@ -14,6 +14,7 @@
 AHEAD = 3
 NORM_ROWS = 16
 MASKED = -1e30
+OUT_ROWS = 48
 VMEM_BYTES = 48 * 1024 * 1024
 EPSILON = 1e-06
 
@@ -249,6 +250,19 @@
         code_message(off, me).wait_send()
 
 
+def write_out(rows, held, out_hbm, sem):
+    pieces = [
+        pltpu.make_async_copy(
+            held.at[0, pl.ds(i * rows, rows)], out_hbm.at[0, pl.ds(i * rows, rows)], sem.at[i]
+        )
+        for i in range(held.shape[1] // rows)
+    ]
+    for piece in pieces:
+        piece.start()
+    for piece in pieces:
+        piece.wait()
+
+
 def shards(n, query_rows, key_rows, value_rows, query_gain, key_gain, tile_lists, tile_counts):
     _, tokens, width = query_rows.shape
     lists = jnp.transpose(tile_lists, (2, 3, 0, 1))
@@ -258,7 +272,7 @@
     groups = width // group_width
     code_rows = -(-block_count // 8) * 8
     visited = tokens * n * tokens * width
-    return pl.pallas_call(
+    attended = pl.pallas_call(
         functools.partial(kernel, n),
         out_shape=pltpu.VMEM(query_rows.shape, jnp.bfloat16),
         in_specs=[pl.BlockSpec(memory_space=pltpu.HBM)] * 7,
@@ -305,6 +319,17 @@
             )
         )
     )
+    rows = math.gcd(tokens, OUT_ROWS)
+    return pl.pallas_call(
+        functools.partial(write_out, rows),
+        out_shape=jax.ShapeDtypeStruct(query_rows.shape, jnp.bfloat16),
+        in_specs=[pl.BlockSpec(memory_space=pltpu.VMEM)],
+        out_specs=pl.BlockSpec(memory_space=pltpu.HBM),
+        scratch_shapes=[pltpu.SemaphoreType.DMA((tokens // rows,))],
+        cost_estimate=pl.CostEstimate(
+            flops=0, bytes_accessed=4 * tokens * width, transcendentals=0
+        ),
+    )(attended)
 
 
 def solution(mesh):

time: 92.7 us -> 95.5 us (1.030)
  Pallas kernels: 91.3 us -> 94.1 us
    pallas_call x0 -> x1, Pallas kernels: none -> 2.84 us  [shards(): pl.pallas_call(functools.partial(write_out, rows), out_shape=jax.ShapeDty...]
where the time goes in v7:
time: 95.5 us; the launch traced here: 95.4 us
  Pallas kernels  94.1 us (99%)
  local copies, waits for them, and re-layouts  1.27 us (1%)
    pallas_call x1, Pallas kernels, shards(): pl.pallas_call(functools.partial(kernel, n), out_shape=pltpu.VMEM(query_r...  91.3 us
    pallas_call x1, Pallas kernels, shards(): pl.pallas_call(functools.partial(write_out, rows), out_shape=jax.ShapeDty...  2.84 us

profile of v7, /device:TPU:0, one launch (start us, length us, event | category | flops | bytes accessed | tf_op | source)
XLA Modules:
  0.0 95.4 jit_solution(2407704509132968745)
XLA Ops:
  0.0 91.3 %shard_map.73.held = bf16[1,192,5120]{2,1,0:T(8,128)(2,1)S(1)} custom-call(bf16[1,192,5120]{2,1,0:T(8,128)(2,1)} %query_hbm.1, bf16[1,192,5120]{2,1,0:T(8,128)(2,1)} %key_hbm.1, bf16[1,192,5120]{2,1,0:T(8,128)(2,1)} %value_hbm.1, f32[1,5120]{1,0:T(1,128)} %bitcast.6, f32[1,5120]{1,0:T(1,128)} %bitcast.7, s32[3,3,16,20]{3,2,1,0:T(8,128)} %bitcast.4, ...), custom_call_target="tpu_custom_call" | custom-call | flops 1509949440 | bytes 7864320 | tf_op jit(solution)/shard_map/pallas_call | solution.py:275
  91.3 0.0 copy-start
  91.3 1.3 %copy-done = bf16[1,192,5120]{2,1,0:T(8,128)(2,1)} copy-done((bf16[1,192,5120]{2,1,0:T(8,128)(2,1)}, bf16[1,192,5120]{2,1,0:T(8,128)(2,1)S(1)}, u32[]{:S(2)}) %copy-start) | copy-done | bytes 1966104
  92.5 2.8 %shard_map.74 = bf16[1,192,5120]{2,1,0:T(8,128)(2,1)} custom-call(bf16[1,192,5120]{2,1,0:T(8,128)(2,1)} %copy-done), custom_call_target="tpu_custom_call" | custom-call | bytes 3932160 | tf_op jit(solution)/shard_map/pallas_call | solution.py:323
Async XLA Ops:
  91.3 1.3 %copy-start = (bf16[1,192,5120]{2,1,0:T(8,128)(2,1)}, bf16[1,192,5120]{2,1,0:T(8,128)(2,1)S(1)}, u32[]{:S(2)}) copy-start(bf16[1,192,5120]{2,1,0:T(8,128)(2,1)S(1)} %shard_map.73.held) | copy-start | bytes 5898244
